TPU v7x, 32 devices: a whole 2x2x4 slice. The times are simulated.
32 devices in a mesh: dp: 8 (over y, x, core), tensor: 4 (over z).
Axes of the slice: x: 2, y: 2, z: 4, core: 2. Of those that a mesh axis runs over, the one named last changes fastest.
Arguments:
- target_hidden: bfloat16 [256, 16384], P('dp', 'tensor'), may hold values from -64 to 64
- target_gain: bfloat16 [16384], replicated, may hold values from 0.25 to 1.75
- target_head: bfloat16 [16384, 65536], P(None, ('dp', 'tensor')), may hold values from -8 to 8
- reference_hidden: bfloat16 [256, 4096], P('dp', 'tensor'), may hold values from -64 to 64
- reference_gain: bfloat16 [4096], replicated, may hold values from 0.25 to 1.75
- reference_head: bfloat16 [4096, 65536], P(None, ('dp', 'tensor')), may hold values from -8 to 8
Outputs:
- contrast: float32 [256, 65536], P(None, ('dp', 'tensor'))
All inputs are finite; a program needn't handle non-finite values.
Results may differ from a plain program's by a relative error of at most 0.0012.
Values may be sent and summed in bfloat16 or wider, within the bound.
A program may use at most 192 MiB of HBM per device.

v0:
```python
import jax
import jax.numpy as jnp
from jax import lax
from jax.sharding import PartitionSpec as P

EPS = 1e-05
LOG_TEN = 2.302585092994046


def normalize_full(piece, gain):
    values = piece.astype(jnp.float32)
    square_mean = jnp.mean(values * values, axis=1, keepdims=True)
    return (values * lax.rsqrt(square_mean + EPS) * gain.astype(jnp.float32)).astype(jnp.bfloat16)


def local(
    target_hidden, target_gain, target_head, reference_hidden, reference_gain, reference_head
):
    wide_t, wide_r = (
        lax.all_gather(target_hidden, "tensor", axis=1, tiled=True),
        lax.all_gather(reference_hidden, "tensor", axis=1, tiled=True),
    )
    logits_t = jnp.dot(
        normalize_full(lax.all_gather(wide_t, "dp", axis=0, tiled=True), target_gain),
        target_head,
        preferred_element_type=jnp.float32,
    )
    logits_r = jnp.dot(
        normalize_full(lax.all_gather(wide_r, "dp", axis=0, tiled=True), reference_gain),
        reference_head,
        preferred_element_type=jnp.float32,
    )
    local_peak_t = jnp.max(logits_t, axis=1)
    local_peak_r = jnp.max(logits_r, axis=1)
    peak_t, peak_r = lax.pmax((local_peak_t, local_peak_r), ("dp", "tensor"))
    local_total_t = jnp.sum(jnp.exp(logits_t - peak_t[:, None]), axis=1)
    local_total_r = jnp.sum(jnp.exp(logits_r - peak_r[:, None]), axis=1)
    total_t, total_r = lax.psum((local_total_t, local_total_r), ("dp", "tensor"))
    lse_t = (peak_t + jnp.log(total_t))[:, None]
    lse_r = (peak_r + jnp.log(total_r))[:, None]
    margin = jnp.minimum(0.0, logits_t - peak_t[:, None] + LOG_TEN)
    return logits_t - lse_t - 0.5 * (logits_r - lse_r) + margin


def solution(mesh):
    placed = (
        P("dp", "tensor"),
        P(),
        P(None, ("dp", "tensor")),
        P("dp", "tensor"),
        P(),
        P(None, ("dp", "tensor")),
    )
    return jax.shard_map(
        local, mesh=mesh, in_specs=placed, out_specs=P(None, ("dp", "tensor")), check_vma=False
    )
```

profile of v0, /device:TPU:0, one launch (start us, length us, event | category | flops | bytes accessed | tf_op | source)
XLA Modules:
  0.0 253.1 jit_solution(15033309289125292821)
XLA Ops:
  6.5 0.0 all-gather.4.cloned.1.call-start
  6.5 0.7 all-gather.4.cloned.1.call-update
  7.3 0.0 all-gather.8.cloned.1.call-start
  7.3 18.5 %all_gather.14 = bf16[32,4096]{1,0:T(8,128)(2,1)} all-gather(bf16[32,1024]{1,0:T(8,128)(2,1)} %param.9), channel_id=1, replica_groups=mesh['dp'=8,'tensor'=4] {'tensor'}, dimensions={1}, use_global_device_ids=true | all-gather | bytes 327680 | tf_op jit(solution)/shard_map/all_gather | solution.py:21
  25.8 0.0 all-gather.8.cloned.1.call-update
  25.8 0.0 all-gather.6.cloned.1.call-start
  25.9 14.3 %all-gather.4.cloned.1.call-done = bf16[32,16384]{1,0:T(8,128)(2,1)} async-done(((bf16[32,4096]{1,0:T(8,128)(2,1)}), bf16[32,16384]{1,0:T(8,128)(2,1)}) %all-gather.4.cloned.1.call-update) | async-done | bytes 1048592 | tf_op jit(solution)/shard_map/all_gather | solution.py:20
  40.2 0.0 all-gather.6.cloned.1.call-update
  40.2 0.7 convert_element_type.22
  40.9 0.8 convert_element_type.19
  41.7 28.0 %all-gather.8.cloned.1.call-done = bf16[256,4096]{1,0:T(8,128)(2,1)} async-done(((bf16[32,4096]{1,0:T(8,128)(2,1)}), bf16[256,4096]{1,0:T(8,128)(2,1)}) %all-gather.8.cloned.1.call-update) | async-done | bytes 2097168 | tf_op jit(solution)/shard_map/all_gather | solution.py:29
  69.7 0.0 copy-start
  69.7 2.2 fusion.7
  71.9 0.0 copy-done
  71.9 8.4 %fusion.14 = (f32[256]{0:T(256)S(1)}, f32[256,2048]{1,0:T(8,128)S(1)}) fusion(bf16[4096,2048]{1,0:T(8,128)(2,1)} %param.11, bf16[256,4096]{1,0:T(8,128)(2,1)S(1)} %copy-done, f32[4096]{0:T(1024)S(1)} %convert_element_type.22, f32[256]{0:T(256)S(1)} %add_rsqrt_fusion), kind=kOutput, calls=%fused_computation.23 | convolution fusion | flops 4299685888 | bytes 20989952 | tf_op jit(solution)/shard_map/dot_general | solution.py:28
  80.4 45.6 %all-gather.6.cloned.1.call-done = bf16[256,16384]{1,0:T(8,128)(2,1)} async-done(((bf16[32,16384]{1,0:T(8,128)(2,1)}), bf16[256,16384]{1,0:T(8,128)(2,1)}) %all-gather.6.cloned.1.call-update) | async-done | bytes 8388624 | tf_op jit(solution)/shard_map/all_gather | solution.py:24
  126.0 5.1 %fusion = f32[256]{0:T(256)S(1)} fusion(bf16[256,16384]{1,0:T(8,128)(2,1)} %all-gather.6.cloned.1.call-done), kind=kLoop, calls=%fused_computation.2 | loop fusion | flops 12582656 | bytes 8389632 | tf_op jit(solution)/shard_map/reduce_sum | solution.py:12
  131.1 29.2 %fusion.15 = (f32[256]{0:T(256)S(1)}, f32[256,2048]{1,0:T(8,128)}) fusion(bf16[16384,2048]{1,0:T(8,128)(2,1)} %param.8, bf16[256,16384]{1,0:T(8,128)(2,1)} %all-gather.6.cloned.1.call-done, f32[16384]{0:T(1024)S(1)} %convert_element_type.19, f32[256]{0:T(256)S(1)} %add_rsqrt_fusion.1), kind=kOutput, calls=%fused_computation.24 | convolution fusion | flops 17197170688 | bytes 77662208 | tf_op jit(solution)/shard_map/dot_general | solution.py:23
  160.3 39.3 %all-reduce.1 = (f32[256]{0:T(256)S(1)}, f32[256]{0:T(256)S(1)}) all-reduce(f32[256]{0:T(256)S(1)} %get-tuple-element.9, f32[256]{0:T(256)S(1)} %get-tuple-element.11), channel_id=1, replica_groups=mesh['dp'=8,'tensor'=4] {'dp','tensor'}, use_global_device_ids=true, to_apply=%region_7.0 | all-reduce | flops 512 | bytes 4096 | tf_op jit(solution)/shard_map/pmax | solution.py:35
  199.7 2.3 exponential_reduce_fusion
  201.9 41.0 %all-reduce = (f32[256]{0:T(256)S(1)}, f32[256]{0:T(256)S(1)}) all-reduce(f32[256]{0:T(256)S(1)} %get-tuple-element.13, f32[256]{0:T(256)S(1)} %get-tuple-element.14), channel_id=1, replica_groups=mesh['dp'=8,'tensor'=4] {'dp','tensor'}, use_global_device_ids=true, to_apply=%region_9.0 | all-reduce | flops 512 | bytes 4096 | tf_op jit(solution)/shard_map/psum | solution.py:38
  243.0 3.6 %minimum_add_fusion = f32[256,2048]{1,0:T(8,128)} fusion(f32[256,2048]{1,0:T(8,128)S(1)} %get-tuple-element.10, f32[256,2048]{1,0:T(8,128)} %get-tuple-element.12, f32[256]{0:T(256)S(1)} %log_add_fusion, f32[256]{0:T(256)S(1)} %log_add_fusion.1, f32[256]{0:T(256)S(1)} %get-tuple-element.8), kind=kLoop, calls=%fused_computation.14 | loop fusion | flops 4194304 | bytes 6294528 | tf_op jit(solution)/shard_map/add | solution.py:42
  (4 shorter events, 0.0 us)
Async XLA Ops:
  6.5 33.7 %all-gather.4.cloned.1.call-start = ((), (), s32[]{:S(2)}) async-start(), calls=%async_computation | async-start | bytes 1310720 | tf_op jit(solution)/shard_map/all_gather | solution.py:20
  7.3 62.4 %all-gather.8.cloned.1.call-start = ((), (), s32[]{:S(2)}) async-start(), calls=%async_computation.2 | async-start | bytes 2359296 | tf_op jit(solution)/shard_map/all_gather | solution.py:29
  25.8 100.2 %all-gather.6.cloned.1.call-start = ((), (), s32[]{:S(2)}) async-start(), calls=%async_computation.1 | async-start | bytes 9437184 | tf_op jit(solution)/shard_map/all_gather | solution.py:24
  69.7 2.2 copy-start
Sparse Core Ops, SparseCore 0:
  8.9 31.2 all-gather.3
  42.1 27.5 all-gather.7
  71.6 54.3 all-gather.5
where the time goes:
time: 254 us; the launch traced here: 253 us
  blocking collectives  98.8 us (39%)
  waiting for transfers between devices  88.7 us (35%)
  matrix products  37.7 us (15%)
  other arithmetic  14.7 us (6%)
  between operations  13.1 us (5%)
    all_gather x1, waiting for transfers between devices, local(): lax.all_gather(wide_t, 'dp', axis=0, tiled=True)  45.6 us
    psum x1, blocking collectives, local(): lax.psum((local_total_t, local_total_r), ('dp', 'tensor'))  41 us
    pmax x1, blocking collectives, local(): peak_t, peak_r = lax.pmax((local_peak_t, local_peak_r), ('dp', 'tensor'))  39.3 us
    dot_general x1, matrix products, local(): jnp.dot(normalize_full(lax.all_gather(wide_t, 'dp', axis=0, tiled=True),...  29.2 us
    all_gather x1, waiting for transfers between devices, local(): lax.all_gather(wide_r, 'dp', axis=0, tiled=True)  28 us
    all_gather x1, blocking collectives, local(): lax.all_gather(reference_hidden, 'tensor', axis=1, tiled=True)  18.5 us
    all_gather x1, waiting for transfers between devices, local(): lax.all_gather(target_hidden, 'tensor', axis=1, tiled=True)  14.3 us
    dot_general x1, matrix products, local(): jnp.dot(normalize_full(lax.all_gather(wide_r, 'dp', axis=0, tiled=True),...  8.45 us
  transfers between devices with their start and end apart: 3, of which 3 were waited for; matrix products, arithmetic and copies ran while one was open for 5% of the time, Pallas kernels for 0%

commit v1 on v0

v1 whole, which is shorter than its diff:
```python
import functools

import jax
import jax.numpy as jnp
from jax import lax
from jax.experimental import pallas as pl
from jax.experimental.pallas import tpu as pltpu
from jax.sharding import PartitionSpec as P

EPS = 1e-05
LOG_TEN = 2.302585092994046
MESH = pl.DeviceIdType.MESH
F32 = jnp.float32


def kernel(
    n_dp, n_t, nw, ht_ref, hr_ref, gain_ref, wt_ref, wr_ref, out_ref,
    normed, heads, acc_t, acc_r, local_stats, squares, squares_in, stat_a, stat_b,
    z_send, z_recv, two_send, two_recv, three_send, three_recv, core_send, core_recv,
    sq_send, sq_recv, a_send, a_recv, b_send, b_recv, head_sem, out_sem,
):
    quads = n_dp // 2
    n_lo, n_hi = 2, quads // 2
    half = normed.shape[3]
    width = normed.shape[4]
    rows = n_dp * 2 * half
    columns = acc_t.shape[1]
    d = lax.axis_index("dp")
    z = lax.axis_index("tensor")
    core = lax.rem(d, 2)
    lo = lax.rem(lax.div(d, 2), n_lo)
    hi = lax.div(d, 2 * n_lo)
    base_a = core * quads
    base_b = n_dp + core * quads
    own_a = base_a + hi * n_lo + lo
    own_b = base_b + lo * n_hi + hi

    def dp_index(high, low, c):
        return (high * n_lo + low) * 2 + c

    sibling = dp_index(hi, lo, 1 - core)
    other_lo = [lax.rem(lo + k, n_lo) for k in range(1, n_lo)]
    other_hi = [lax.rem(hi + k, n_hi) for k in range(1, n_hi)]
    other_z = [lax.rem(z + k, n_t) for k in range(1, n_t)]
    other_d = [lax.rem(d + k, n_dp) for k in range(1, n_dp)]

    def send(src, dst, send_sem, recv_sem, dev):
        pltpu.make_async_remote_copy(
            src_ref=src, dst_ref=dst, send_sem=send_sem, recv_sem=recv_sem,
            device_id=dev, device_id_type=MESH,
        ).start()

    def push(view, send_sem, recv_sem, dev):
        send(view, view, send_sem, recv_sem, dev)

    def await_bytes(view, sem):
        pltpu.make_async_copy(view, view, sem).wait()

    def head_copy(j, i):
        slot = j % 2
        if j == 0:
            src = wr_ref.at[pl.ds(pl.multiple_of(i * width, width), width), :]
        else:
            src = wt_ref.at[pl.ds(pl.multiple_of((i * (nw - 1) + j - 1) * width, width), width), :]
        return pltpu.make_async_copy(src, heads.at[slot, i], head_sem.at[slot, i])

    def start_heads(j):
        def body(i, _):
            head_copy(j, i).start()
            return 0
        lax.fori_loop(0, n_t, body, 0)

    start_heads(0)
    start_heads(1)

    barrier = pltpu.get_barrier_semaphore()
    for t in other_z:
        pl.semaphore_signal(barrier, inc=1, device_id=(d, t), device_id_type=MESH)
    for p in other_d:
        pl.semaphore_signal(barrier, inc=1, device_id=(p, z), device_id_type=MESH)

    vt = ht_ref[...].astype(F32)
    vr = hr_ref[...].astype(F32)
    st = jnp.sum(vt * vt, axis=1, keepdims=True)
    sr = jnp.sum(vr * vr, axis=1, keepdims=True)
    lane = lax.broadcasted_iota(jnp.int32, squares.shape, 1)
    squares[...] = jnp.where(lane < 64, st, sr)
    squares_in[z] = squares[...]
    pl.semaphore_wait(barrier, n_t + n_dp - 2)
    for t in other_z:
        send(squares, squares_in.at[z], sq_send, sq_recv, (d, t))
    await_bytes(squares_in.at[pl.ds(0, n_t - 1)], sq_recv)
    total_sq = squares_in[0]
    for k in range(1, n_t):
        total_sq = total_sq + squares_in[k]
    scale_t = lax.rsqrt(total_sq[:, 0:1] / F32(width * (nw - 1) * n_t) + EPS)
    scale_r = lax.rsqrt(total_sq[:, 64:65] / F32(width * n_t) + EPS)

    def normalize(j):
        gain = gain_ref[:, j * width:(j + 1) * width]
        if j == 0:
            part, scale = hr_ref[...], scale_r
        else:
            part, scale = ht_ref[:, (j - 1) * width:j * width], scale_t
        value = (part.astype(F32) * scale * gain).astype(jnp.bfloat16)
        normed[j, z, own_a] = value[:half]
        normed[j, z, own_b] = value[half:]

    def start_z(j):
        for t in other_z:
            push(normed.at[j, z, own_a], z_send, z_recv.at[j], (d, t))
            push(normed.at[j, z, own_b], z_send, z_recv.at[j], (d, t))

    def to_core(view, j):
        push(view, core_send, core_recv.at[j], (sibling, z))

    def start_two(j):
        for x in other_lo:
            push(normed.at[j, :, own_a], two_send, two_recv.at[j], (dp_index(hi, x, core), z))
        for y in other_hi:
            push(normed.at[j, :, own_b], two_send, two_recv.at[j], (dp_index(y, lo, core), z))
        to_core(normed.at[j, :, own_a], j)
        to_core(normed.at[j, :, own_b], j)

    def start_three(j):
        for y in other_hi:
            push(normed.at[j, :, pl.ds(base_a + hi * n_lo, n_lo)], three_send, three_recv.at[j],
                 (dp_index(y, lo, core), z))
        for x in other_lo:
            push(normed.at[j, :, pl.ds(base_b + lo * n_hi, n_hi)], three_send, three_recv.at[j],
                 (dp_index(hi, x, core), z))
        for x in other_lo:
            to_core(normed.at[j, :, base_a + hi * n_lo + x], j)
        for y in other_hi:
            to_core(normed.at[j, :, base_b + lo * n_hi + y], j)

    def finish_three(j):
        for y in other_hi:
            to_core(normed.at[j, :, pl.ds(base_a + y * n_lo, n_lo)], j)
        for x in other_lo:
            to_core(normed.at[j, :, pl.ds(base_b + x * n_hi, n_hi)], j)

    tile = min(512, columns)

    def multiply(j):
        acc = acc_r if j == 0 else acc_t

        def one(i, _):
            head_copy(j, i).wait()

            def part(n, _):
                cols = pl.ds(pl.multiple_of(n * tile, tile), tile)
                product = jnp.dot(
                    normed[j, i].reshape(rows, width), heads[j % 2, i, :, cols],
                    preferred_element_type=F32,
                )
                acc[:, cols] += product
                return 0

            lax.fori_loop(0, columns // tile, part, 0)
            if j + 2 < nw:
                head_copy(j + 2, i).start()
            return 0

        acc[...] = jnp.zeros_like(acc)if j < 2 else acc[...]
        lax.fori_loop(0, n_t, one, 0)

    lanes = lax.broadcasted_iota(jnp.int32, (half, 128), 1)

    def row_stats(acc, first):
        def body(b, _):
            r = pl.ds(pl.multiple_of(b * half, half), half)
            v = acc[r, :]
            peak = jnp.max(v, axis=1, keepdims=True)
            total = jnp.sum(jnp.exp(v - peak), axis=1, keepdims=True)
            old = local_stats[r, :]
            local_stats[r, :] = jnp.where(
                lanes == first, peak, jnp.where(lanes == first + 1, total, old)
            )
            return 0

        lax.fori_loop(0, 2 * n_dp, body, 0)

    local_stats[...] = jnp.zeros_like(local_stats)
    normalize(0)
    start_z(0)
    for j in range(1, nw):
        normalize(j)

    for s in range(nw + 3):
        if 0 <= s - 1 < nw:
            j = s - 1
            await_bytes(normed.at[j, :, pl.ds(0, n_lo + n_hi - 2)], two_recv.at[j])
            start_three(j)
        if s < nw:
            await_bytes(normed.at[s, pl.ds(0, n_t - 1), pl.ds(0, 2)], z_recv.at[s])
            start_two(s)
            if s + 1 < nw:
                start_z(s + 1)
        if 0 <= s - 3 < nw:
            j = s - 3
            await_bytes(normed.at[j, :, pl.ds(0, n_dp)], core_recv.at[j])
            multiply(j)
            if j == 0:
                row_stats(acc_r, 2)
        if 0 <= s - 2 < nw:
            j = s - 2
            await_bytes(
                normed.at[j, :, pl.ds(0, n_lo * (n_hi - 1) + n_hi * (n_lo - 1))], three_recv.at[j]
            )
            finish_three(j)

    row_stats(acc_t, 0)

    def combine(parts):
        peak_t, total_t, peak_r, total_r = (
            [p[k:k + 1, :] for p in parts] for k in range(4)
        )
        top_t = functools.reduce(jnp.maximum, peak_t)
        top_r = functools.reduce(jnp.maximum, peak_r)
        sum_t = sum(t * jnp.exp(p - top_t) for p, t in zip(peak_t, total_t))
        sum_r = sum(t * jnp.exp(p - top_r) for p, t in zip(peak_r, total_r))
        return top_t, sum_t, top_r, sum_r

    def stack(values):
        row = lax.broadcasted_iota(jnp.int32, (8, rows), 0)
        result = jnp.zeros((8, rows), F32)
        for k, v in enumerate(values):
            result = jnp.where(row == k, v, result)
        return result

    stat_a[z] = jnp.transpose(local_stats[...])[0:8, :]
    for t in other_z:
        push(stat_a.at[z], a_send, a_recv, (d, t))
    await_bytes(stat_a.at[pl.ds(0, n_t - 1)], a_recv)
    stat_b[d] = stack(combine([stat_a[k] for k in range(n_t)]))
    for p in other_d:
        push(stat_b.at[d], b_send, b_recv, (p, z))
    await_bytes(stat_b.at[pl.ds(0, n_dp - 1)], b_recv)
    top_t, sum_t, top_r, sum_r = combine([stat_b[k] for k in range(n_dp)])
    lse_t = top_t + jnp.log(sum_t)
    lse_r = top_r + jnp.log(sum_r)
    final = stack((top_t, lse_t, lse_r))
    local_stats[...] = jnp.transpose(
        jnp.concatenate([final, jnp.zeros((120, rows), F32)], axis=0)
    )

    def finish(b, place):
        r = pl.ds(pl.multiple_of(b * half, half), half)
        stats = local_stats[r, :]
        lt = acc_t[r, :]
        margin = jnp.minimum(0.0, lt - stats[:, 0:1] + LOG_TEN)
        acc_t[r, :] = lt - stats[:, 1:2] - 0.5 * (acc_r[r, :] - stats[:, 2:3]) + margin
        pltpu.make_async_copy(
            acc_t.at[r, :], out_ref.at[pl.ds(pl.multiple_of(place * half, half), half), :], out_sem
        ).start()

    def finish_a(b, _):
        c, q = b // quads, b % quads
        finish(b, (q * 2 + c) * 2)
        return 0

    def finish_b(b, _):
        c, q = b // quads, b % quads
        low, high = q // n_hi, q % n_hi
        finish(n_dp + b, dp_index(high, low, c) * 2 + 1)
        return 0

    lax.fori_loop(0, n_dp, finish_a, 0)
    lax.fori_loop(0, n_dp, finish_b, 0)

    await_bytes(squares_in.at[pl.ds(0, n_t - 1)], sq_send)
    await_bytes(normed.at[:, pl.ds(0, n_t - 1), pl.ds(0, 2)], z_send)
    await_bytes(normed.at[:, :, pl.ds(0, n_lo + n_hi - 2)], two_send)
    await_bytes(
        normed.at[:, :, pl.ds(0, n_lo * (n_hi - 1) + n_hi * (n_lo - 1))], three_send
    )
    await_bytes(normed.at[:, :, pl.ds(0, n_dp)], core_send)
    await_bytes(stat_a.at[pl.ds(0, n_t - 1)], a_send)
    await_bytes(stat_b.at[pl.ds(0, n_dp - 1)], b_send)
    await_bytes(acc_t, out_sem)


def local(n_dp, n_t, target_hidden, target_gain, target_head, reference_hidden, reference_gain, reference_head):
    rows, wide = target_hidden.shape
    width = reference_hidden.shape[1]
    nw = wide // width + 1
    columns = target_head.shape[1]
    half = rows // 2
    z = lax.axis_index("tensor")
    gain = jnp.concatenate(
        [
            lax.dynamic_slice(reference_gain, (z * width,), (width,)),
            lax.dynamic_slice(target_gain, (z * wide,), (wide,)),
        ]
    ).astype(F32)[None, :]
    dma = pltpu.SemaphoreType.DMA
    vmem = pl.BlockSpec(memory_space=pltpu.VMEM)
    hbm = pl.BlockSpec(memory_space=pl.ANY)
    all_rows = rows * n_dp
    depth = target_head.shape[0] + reference_head.shape[0]
    return pl.pallas_call(
        functools.partial(kernel, n_dp, n_t, nw),
        out_shape=jax.ShapeDtypeStruct((all_rows, columns), F32),
        in_specs=[vmem, vmem, vmem, hbm, hbm],
        out_specs=hbm,
        scratch_shapes=[
            pltpu.VMEM((nw, n_t, 2 * n_dp, half, width), jnp.bfloat16),
            pltpu.VMEM((2, n_t, width, columns), jnp.bfloat16),
            pltpu.VMEM((all_rows, columns), F32),
            pltpu.VMEM((all_rows, columns), F32),
            pltpu.VMEM((all_rows, 128), F32),
            pltpu.VMEM((rows, 128), F32),
            pltpu.VMEM((n_t, rows, 128), F32),
            pltpu.VMEM((n_t, 8, all_rows), F32),
            pltpu.VMEM((n_dp, 8, all_rows), F32),
            dma, dma((nw,)), dma, dma((nw,)), dma, dma((nw,)), dma, dma((nw,)),
            dma, dma, dma, dma, dma, dma, dma((2, n_t)), dma,
        ],
        compiler_params=pltpu.CompilerParams(
            collective_id=0, has_side_effects=True, vmem_limit_bytes=58 * 2**20
        ),
        cost_estimate=pl.CostEstimate(
            flops=2 * all_rows * depth * columns,
            bytes_accessed=2 * depth * columns,
            transcendentals=2 * all_rows * columns,
        ),
    )(target_hidden, reference_hidden, gain, target_head, reference_head)


def solution(mesh):
    placed = (
        P("dp", "tensor"),
        P(),
        P(None, ("dp", "tensor")),
        P("dp", "tensor"),
        P(),
        P(None, ("dp", "tensor")),
    )
    return jax.shard_map(
        functools.partial(local, mesh.shape["dp"], mesh.shape["tensor"]),
        mesh=mesh, in_specs=placed, out_specs=P(None, ("dp", "tensor")), check_vma=False,
    )
```

time: 254 us -> 105 us (0.41)
  Pallas kernels: 0 us -> 99.9 us
  blocking collectives: 98.8 us -> 0 us
  waiting for transfers between devices: 88.7 us -> 0 us
  matrix products: 37.7 us -> 0 us
  other arithmetic: 14.7 us -> 0.63 us
  between operations: 13.1 us -> 0.01 us
  local copies, waits for them, and re-layouts: 0.01 us -> 4.54 us
    pallas_call x0 -> x1, Pallas kernels: none -> 99.9 us  [local(): pl.pallas_call(functools.partial(kernel, n_dp, n_t, nw), out_shape=jax.Sh...]
    all_gather x3 -> x0, waiting for transfers between devices: 87.9 us -> none  [the longest x1 45.6 us: local(): lax.all_gather(wide_t, 'dp', axis=0, tiled=True)]
    psum x1 -> x0, blocking collectives: 41 us -> none  [local(): lax.psum((local_total_t, local_total_r), ('dp', 'tensor'))]
    pmax x1 -> x0, blocking collectives: 39.3 us -> none  [local(): peak_t, peak_r = lax.pmax((local_peak_t, local_peak_r), ('dp', 'tensor'))]
    dot_general x2 -> x0, matrix products: 37.7 us -> none  [the longest x1 29.2 us: local(): jnp.dot(normalize_full(lax.all_gather(wide_t, 'dp', axis=0, tiled=True),...]
    all_gather x1 -> x0, blocking collectives: 18.5 us -> none  [local(): lax.all_gather(reference_hidden, 'tensor', axis=1, tiled=True)]
    reduce_sum x3 -> x0, other arithmetic: 9.66 us -> none  [the longest x2 7.37 us: normalize_full(): square_mean = jnp.mean(values * values, axis=1, keepdims=True)]
    add x3 -> x0, other arithmetic: 3.56 us -> none  [the longest x1 3.55 us: local(): return logits_t - lse_t - 0.5 * (logits_r - lse_r) + margin]
  transfers between devices with their start and end apart: 3 -> 0, of which waited for: 3 -> 0; matrix products, arithmetic and copies ran while one was open for 5% -> 0% of each run, Pallas kernels for 0% -> 0%
where the time goes in v1:
time: 105 us
  Pallas kernels  99.9 us (95%)
  local copies, waits for them, and re-layouts  4.54 us (4%)
    pallas_call x1, Pallas kernels, local(): pl.pallas_call(functools.partial(kernel, n_dp, n_t, nw), out_shape=jax.Sh...  99.9 us
    unnamed x1, local copies, waits for them, and re-layouts  3.14 us

profile of v1, /device:TPU:0, one launch (start us, length us, event | category | flops | bytes accessed | tf_op | source)
XLA Modules:
  0.0 105.1 jit_solution(7205635985569290142)
XLA Ops:
  0.0 0.7 dynamic_slice.6
  0.7 0.7 dynamic_slice.7
  1.4 0.6 maximum_convert_fusion.gain_ref
  2.0 99.9 %shard_map.64 = f32[256,2048]{1,0:T(8,128)} custom-call(bf16[32,4096]{1,0:T(8,128)(2,1)} %ht_ref.1, bf16[32,1024]{1,0:T(8,128)(2,1)} %hr_ref.1, f32[1,5120]{1,0:T(1,128)} %maximum_convert_fusion.gain_ref, bf16[16384,2048]{1,0:T(8,128)(2,1)} %wt_ref.1, bf16[4096,2048]{1,0:T(8,128)(2,1)} %wr_ref.1), custom_call_target="tpu_custom_call" | custom-call | flops 21474836480 | bytes 83886080 | tf_op jit(solution)/shard_map/pallas_call | solution.py:302
  102.0 3.1 %copy.8 = f32[256,2048]{1,0:T(8,128)} copy(f32[256,2048]{1,0:T(8,128)} %shard_map.64) | data formatting | bytes 4194304
  (2 shorter events, 0.0 us)
